TPU v7x, 128 devices: a whole 4x4x4 slice. The times are simulated.
128 devices in a mesh: seq: 32 (over y, z, core), head: 4 (over x).
Axes of the slice: x: 4, y: 4, z: 4, core: 2. Of those that a mesh axis runs over, the one named last changes fastest.
Arguments:
- tile_features: bfloat16 [81920, 768], P(('seq', 'head')), may hold values from -40 to 40
- kept_tiles: int32 [32768], P('seq'), may hold values from 0 to 81919, as said below
- attn_gain: float32 [768], replicated, may hold values from 0.1 to 1.9
- qkv_weight: bfloat16 [768, 3, 768], P(None, None, 'head'), may hold values from -4 to 4
- out_weight: bfloat16 [768, 768], P('head'), may hold values from -0.21875 to 0.21875
- middle_head_offset: int32 [12], P('head'), may hold values from 0 to 3
- far_head_offset: int32 [12], P('head'), may hold values from 0 to 15
- mlp_gain: float32 [768], replicated, may hold values from 0.1 to 1.9
- up_weight: bfloat16 [768, 3072], P(None, 'head'), may hold values from -0.21875 to 0.21875
- down_weight: bfloat16 [3072, 768], P('head'), may hold values from -0.109375 to 0.109375
Outputs:
- encoded: bfloat16 [32768, 768], P(('seq', 'head'))
Inputs may be any that keep to these rules, and one draw needn't show every extreme that they name: `kept_tiles`: strictly increasing. For every d < 32, entry (d + 1) * 1024 - 1 minus entry d * 1024 is at most 2047, and equals it for some d.
All inputs are finite; a program needn't handle non-finite values.
Results may differ from a plain program's by a relative error of at most 0.014.
Values may be sent and summed in bfloat16 or wider, within the bound.
A program may use at most 64 MiB of HBM per device.

v0:
```python
import functools

import jax
import jax.numpy as jnp
from jax import lax
from jax.experimental import pallas as pl
from jax.experimental.pallas import tpu as pltpu
from jax.sharding import PartitionSpec as P

NS = 32
NH = 4
ND = NS * NH
D = 768
KD = 1024
HD = 64
HPD = 3
WIN = 16
ROWS = 640
SHARE = KD // NH
EPS = 1e-05
NEG = -1e30
BF = jnp.bfloat16
F32 = jnp.float32


def dot(a, b):
    return lax.dot_general(a, b, (((1,), (0,)), ((), ())), preferred_element_type=F32)


def dot_nt(a, b):
    return lax.dot_general(a, b, (((1,), (1,)), ((), ())), preferred_element_type=F32)


def layer_norm(x, gain):
    centred = x - jnp.mean(x, axis=-1, keepdims=True)
    variance = jnp.mean(centred * centred, axis=-1, keepdims=True)
    return centred * lax.rsqrt(variance + EPS) * gain


def iota(shape, axis):
    return lax.broadcasted_iota(jnp.int32, shape, axis)


def v_first(head):
    return head != 1


def kernel(
    kept_s, moff, foff, kept_c, feat, again, wqkv, mgain, up, down, outw,
    o_ref,
    send, recv, slot, dense, q, kv, qmid, qfar, midkv, farkv, acc, accm, accf,
    ho_send, ho_recv, fk_send, fk_recv, upf, downf, outf,
    fk_ss, fk_rs, s1_ss, s1_rs, xs, xr, ws, wr, wl, ms, mr, fs, fr, hs, hr,
):
    me = lax.axis_index("seq")
    h = lax.axis_index("head")
    right, left, opp = (h + 1) % NH, (h + 3) % NH, (h + 2) % NH
    core = me % 2
    chip = me // 2
    sib = me + 1 - 2 * core
    zbit = chip % 2
    zpart = me + 2 - 4 * zbit
    source = me * NH + h

    def rcopy(src, dst, ssem, rsem, seq, head):
        return pltpu.make_async_remote_copy(
            src_ref=src, dst_ref=dst, send_sem=ssem, recv_sem=rsem,
            device_id=(seq, head), device_id_type=pl.DeviceIdType.MESH,
        )

    barrier = pltpu.get_barrier_semaphore()

    def greet(i, c):
        pl.semaphore_signal(barrier, inc=1, device_id=((me + i) % NS, h), device_id_type=pl.DeviceIdType.MESH)
        return c

    lax.fori_loop(1, NS, greet, 0)
    for other in (right, left, opp):
        pl.semaphore_signal(barrier, inc=1, device_id=(me, other), device_id_type=pl.DeviceIdType.MESH)
    first = kept_s[0]
    fk_send[...] = jnp.full((8, 128), first, jnp.int32)
    fk_recv[0] = fk_send[...]
    pl.semaphore_wait(barrier, NS - 1 + NH - 1)

    def send_first(i, c):
        rcopy(fk_send, fk_recv.at[NS - i], fk_ss, fk_rs, (me + i) % NS, h).start()
        return c

    lax.fori_loop(1, NS, send_first, 0)

    weights = []
    for a, (inp, full) in enumerate(((outw, outf), (up, upf), (down, downf))):
        n = inp.shape[0]
        half, quarter = n // 2, n // 4
        lo = pl.multiple_of(core * half, 16)
        mid = pl.multiple_of(core * half + quarter, 16)
        own = pl.ds(lo, half)
        src = inp.at[own]
        local = pltpu.make_async_copy(inp, full.at[h], wl.at[a])
        mine = [
            rcopy(src, full.at[h, own], ws.at[a, 0], wr.at[a, 0], me, right),
            rcopy(src, full.at[h, own], ws.at[a, 1], wr.at[a, 1], me, left),
        ]
        ahead = [
            rcopy(full.at[left, pl.ds(lo, quarter)], full.at[left, pl.ds(lo, quarter)], ws.at[a, 2], wr.at[a, 2], me, right),
            rcopy(full.at[right, pl.ds(mid, quarter)], full.at[right, pl.ds(mid, quarter)], ws.at[a, 3], wr.at[a, 3], me, left),
        ]
        twin = [
            rcopy(full.at[left, own], full.at[left, own], ws.at[a, 4], wr.at[a, 4], sib, h),
            rcopy(full.at[right, own], full.at[right, own], ws.at[a, 5], wr.at[a, 5], sib, h),
            rcopy(full.at[opp, own], full.at[opp, own], ws.at[a, 6], wr.at[a, 6], sib, h),
        ]
        weights.append((local, mine, ahead, twin))

    def weights_start(a):
        local, mine, _, _ = weights[a]
        local.start()
        mine[0].start()
        mine[1].start()

    def weights_pass(a):
        _, mine, ahead, twin = weights[a]
        for k in range(2):
            mine[k].wait_recv()
            ahead[k].start()
            twin[k].start()

    def weights_last(a):
        _, _, ahead, twin = weights[a]
        ahead[0].wait_recv()
        ahead[1].wait_recv()
        twin[2].start()

    def weights_done(a):
        local, mine, ahead, twin = weights[a]
        for t in twin:
            t.wait_recv()
        local.wait()
        for t in mine + ahead + twin:
            t.wait_send()

    weights_start(0)

    kc = kept_c[...]
    sender = kc & (ND - 1)
    s_seq, s_head = lax.shift_right_arithmetic(sender, 2), sender & (NH - 1)
    within = lax.shift_right_arithmetic(kc, 7) - lax.shift_right_arithmetic(first - sender + (ND - 1), 7)
    rel = (me - s_seq + NS) & (NS - 1)
    slot[...] = (lax.shift_right_arithmetic(rel, 3) * 32 + s_head * 8 + (rel & 7)) * WIN + within

    all_first = rcopy(fk_recv.at[pl.ds(1, NS - 1)], fk_recv.at[pl.ds(1, NS - 1)], fk_ss, fk_rs, me, right)
    all_first.wait_recv()

    def send_windows(g, c):
        firsts = fk_recv[pl.ds(pl.multiple_of(g * 8, 8), 8)]
        start = lax.shift_right_arithmetic(firsts - source + (ND - 1), 7)
        start = jnp.concatenate([start, start], axis=1).reshape(128, 128)
        want = start + iota((128, 128), 0) % WIN - iota((128, 128), 1)
        pick = jnp.concatenate(
            [(want == t * 128).astype(F32).astype(BF) for t in range(ROWS // 128)], axis=1
        )
        send[pl.ds(pl.multiple_of(g * 128, 128), 128)] = dot(pick, feat[...]).astype(BF)

        def one(i, c):
            at = pl.ds(pl.multiple_of(g * 128 + i * WIN, WIN), WIN)
            rcopy(
                send.at[at], recv.at[g, h, pl.ds(pl.multiple_of(i * WIN, WIN), WIN)],
                s1_ss, s1_rs.at[g], (me + g * 8 + i) % NS, h,
            ).start()
            return c

        lax.fori_loop(jnp.where(g == 0, 1, 0), 8, one, 0)
        return c

    lax.fori_loop(0, 4, send_windows, 0)
    recv[0, h, 0:WIN] = send[0:WIN]

    def arrive(g):
        lo = WIN if g == 0 else 0
        part = recv.at[g, h, pl.ds(lo, 128 - lo)]
        rcopy(part, part, s1_ss, s1_rs.at[g], me, right).wait_recv()

    rings = []
    for g in range(4):
        rings.append((
            rcopy(recv.at[g, h], recv.at[g, h], xs.at[g, 0], xr.at[g, 0], me, right),
            rcopy(recv.at[g, h], recv.at[g, h], xs.at[g, 1], xr.at[g, 1], me, left),
            rcopy(recv.at[g, left, pl.ds(0, 64)], recv.at[g, left, pl.ds(0, 64)], xs.at[g, 2], xr.at[g, 2], me, right),
            rcopy(recv.at[g, right, pl.ds(64, 64)], recv.at[g, right, pl.ds(64, 64)], xs.at[g, 3], xr.at[g, 3], me, left),
        ))

    def compact(g):
        rings[g][2].wait_recv()
        rings[g][3].wait_recv()

        def block(b, c):
            at = pl.ds(pl.multiple_of(b * 256, 256), 256)
            pick = (iota((256, 512), 1) + g * 512 == slot[at]).astype(F32).astype(BF)
            got = dot(pick, recv[g].reshape(512, D))
            if g == 0:
                dense[at] = got
            else:
                dense[at] = dense[at] + got
            return c

        lax.fori_loop(0, KD // 256, block, 0)

    def ring_pass(g):
        rings[g][0].wait_recv()
        rings[g][2].start()
        rings[g][1].wait_recv()
        rings[g][3].start()

    for g in range(4):
        arrive(g)
        rings[g][0].start()
        rings[g][1].start()
        if g >= 1:
            ring_pass(g - 1)
    ring_pass(3)
    weights_pass(0)
    weights_start(1)
    weights_start(2)
    for g in range(4):
        compact(g)
    weights_last(0)

    def project(b, c):
        at = pl.ds(pl.multiple_of(b * 256, 256), 256)
        normed = layer_norm(dense[at], again[...]).astype(BF)
        qb = (dot(normed, wqkv[:, :384]).astype(BF).astype(F32) * 0.125).astype(BF)
        kvb = dot(normed, wqkv[:, 384:]).astype(BF)
        q[at] = qb
        kv[at] = kvb
        at_m = pl.ds(pl.multiple_of(b * 64, 64), 64)
        at_f = pl.ds(pl.multiple_of(b * 16, 16), 16)
        for j in range(HPD):
            cols = slice(j * 128, (j + 1) * 128)
            sel = (iota((64, 256), 1) == iota((64, 256), 0) * 4 + moff[j]).astype(F32).astype(BF)
            midkv[core, zbit, at_m, cols] = dot(sel, kvb[:, cols]).astype(BF)
            qmid[at_m, cols] = dot(sel, qb[:, cols]).astype(BF)
            sel = (iota((16, 256), 1) == iota((16, 256), 0) * 16 + foff[j]).astype(F32).astype(BF)
            farkv[core, chip, at_f, cols] = dot(sel, kvb[:, cols]).astype(BF)
            qfar[at_f, cols] = dot(sel, qb[:, cols]).astype(BF)
        return c

    lax.fori_loop(0, KD // 256, project, 0)

    def send_far(i, c):
        rcopy(farkv.at[core, chip], farkv.at[core, chip], fs.at[0], fr.at[0], (me + 2 * i) % NS, h).start()
        return c

    lax.fori_loop(1, NS // 2, send_far, 0)
    mid_z = rcopy(midkv.at[core, zbit], midkv.at[core, zbit], ms.at[0], mr.at[0], zpart, h)
    mid_z.start()
    mid_s = rcopy(midkv.at[core], midkv.at[core], ms.at[1], mr.at[1], sib, h)
    far_all = rcopy(farkv.at[core, pl.ds(0, 15)], farkv.at[core, pl.ds(0, 15)], fs.at[0], fr.at[0], sib, h)
    far_s = rcopy(farkv.at[core], farkv.at[core], fs.at[1], fr.at[1], sib, h)

    def attend(qb, keys, j):
        scores = dot_nt(qb, keys)
        top = jnp.max(scores, axis=-1, keepdims=True)
        p = jnp.exp(scores - top)
        total = jnp.sum(p, axis=-1, keepdims=True)
        out = dot(p.astype(BF), keys)
        lane = iota(out.shape, 1)
        base = 64 if v_first(j) else 0
        out = jnp.where((lane >= base) & (lane < base + 32), top, out)
        return jnp.where((lane >= base + 32) & (lane < base + 64), total, out)

    for j in range(HPD):
        cols = slice(j * 128, (j + 1) * 128)

        def short(b, c):
            at = pl.ds(pl.multiple_of(b * 256, 256), 256)
            acc[j, at] = attend(q[at, cols], kv[:, cols], j)
            return c

        lax.fori_loop(0, KD // 256, short, 0)
        if j == 0:
            mid_z.wait_recv()
            mid_s.start()
        if j == 1:
            far_all.wait_recv()
            far_s.start()
    weights_pass(1)
    mid_s.wait_recv()
    for j in range(HPD):
        cols = slice(j * 128, (j + 1) * 128)
        accm[j] = attend(qmid[:, cols], midkv[:, :, :, cols].reshape(KD, 128), j)
    far_s.wait_recv()
    for j in range(HPD):
        cols = slice(j * 128, (j + 1) * 128)
        accf[j] = attend(qfar[:, cols], farkv[:, :, :, cols].reshape(2048, 128), j)

    def spread(one_hot, x):
        one = x.astype(BF)
        rest = x - one.astype(F32)
        two = rest.astype(BF)
        three = (rest - two.astype(F32)).astype(BF)
        return dot(one_hot, one) + dot(one_hot, two) + dot(one_hot, three)

    def merge(g):
        heads = []
        at = pl.ds(pl.multiple_of(g * 256, 256), 256)
        at_m = pl.ds(pl.multiple_of(g * 64, 64), 64)
        at_f = pl.ds(pl.multiple_of(g * 16, 16), 16)
        for j in range(HPD):
            base = 64 if v_first(j) else 0
            near = acc[j, at]
            hot_m = (iota((256, 64), 0) == iota((256, 64), 1) * 4 + moff[j]).astype(F32).astype(BF)
            hot_f = (iota((256, 16), 0) == iota((256, 16), 1) * 16 + foff[j]).astype(F32).astype(BF)
            middle = spread(hot_m, accm[j, at_m])
            far = spread(hot_f, accf[j, at_f])
            pos = iota((256, 1), 0)
            in_m = pos % 4 == moff[j]
            in_f = pos % 16 == foff[j]
            top_n = near[:, base:base + 1]
            top_m = jnp.where(in_m, middle[:, base:base + 1], NEG)
            top_f = jnp.where(in_f, far[:, base:base + 1], NEG)
            top = jnp.maximum(jnp.maximum(top_n, top_m), top_f)
            c_n = jnp.exp(top_n - top)
            c_m = jnp.exp(top_m - top)
            c_f = jnp.exp(top_f - top)
            under = (
                c_n * near[:, base + 32:base + 33]
                + c_m * middle[:, base + 32:base + 33]
                + c_f * far[:, base + 32:base + 33]
            )
            heads.append((c_n * near + c_m * middle + c_f * far) / under)
        lane = iota((256, 128), 1)
        lower = jnp.where(lane < 64, heads[0], heads[1])
        upper = jnp.where(lane < 64, heads[2], 0.0)
        return jnp.concatenate([lower, upper], axis=1).astype(BF)

    swaps = []
    for r, g in enumerate((right, opp, left)):
        ho_send[r] = merge(g)
        swap = rcopy(ho_send.at[r], ho_recv.at[h], hs.at[r], hr.at[r], me, g)
        swap.start()
        swaps.append(swap)
    ho_recv[h] = merge(h)
    weights_done(0)
    weights_last(1)
    for swap in swaps:
        swap.wait_recv()
    attended = jnp.zeros((SHARE, D), F32)
    for g in range(NH):
        attended = attended + dot(ho_recv[g, :, :192], outf[g]).astype(BF).astype(F32)
    residual = dense[pl.ds(pl.multiple_of(h * SHARE, SHARE), SHARE)] + attended
    normed_two = layer_norm(residual, mgain[...]).astype(BF)
    weights_pass(2)
    weights_done(1)
    weights_last(2)
    weights_done(2)

    def feed(g, total):
        hidden = dot(normed_two, upf[g])
        hidden = (0.5 * hidden * (1.0 + lax.erf(hidden * 0.7071067811865476))).astype(BF)
        return total + dot(hidden, downf[g]).astype(BF).astype(F32)

    o_ref[...] = (residual + lax.fori_loop(0, NH, feed, jnp.zeros((SHARE, D), F32))).astype(BF)

    all_first.wait_send()
    sent = send.at[pl.ds(WIN, (NS - 1) * WIN)]
    rcopy(sent, sent, s1_ss, s1_rs.at[0], me, right).wait_send()
    for ring in rings:
        for copy in ring:
            copy.wait_send()
    far_all.wait_send()
    far_s.wait_send()
    mid_z.wait_send()
    mid_s.wait_send()
    for swap in swaps:
        swap.wait_send()


def local(tile_features, kept_tiles, attn_gain, qkv_weight, out_weight, middle_head_offset,
          far_head_offset, mlp_gain, up_weight, down_weight):
    parts = qkv_weight.reshape(D, 3, HPD, HD)
    zero = jnp.zeros((D, HD), BF)
    columns = []
    for j in range(HPD):
        columns += [zero, parts[:, 0, j]] if v_first(j) else [parts[:, 0, j], zero]
    for j in range(HPD):
        columns += [parts[:, 2, j], parts[:, 1, j]] if v_first(j) else [parts[:, 1, j], parts[:, 2, j]]
    wqkv = jnp.concatenate(columns, axis=1)
    vmem = pl.BlockSpec(memory_space=pltpu.VMEM)
    smem = pl.BlockSpec(memory_space=pltpu.SMEM)
    hbm = pl.BlockSpec(memory_space=pl.ANY)
    dma = pltpu.SemaphoreType.DMA
    return pl.pallas_call(
        kernel,
        out_shape=jax.ShapeDtypeStruct((SHARE, D), BF),
        in_specs=[smem, smem, smem, vmem, vmem, vmem, vmem, vmem, hbm, hbm, hbm],
        out_specs=vmem,
        scratch_shapes=[
            pltpu.VMEM((NS * WIN, D), BF),
            pltpu.VMEM((4, NH, 128, D), BF),
            pltpu.VMEM((KD, 1), jnp.int32),
            pltpu.VMEM((KD, D), F32),
            pltpu.VMEM((KD, 384), BF),
            pltpu.VMEM((KD, 384), BF),
            pltpu.VMEM((256, 384), BF),
            pltpu.VMEM((64, 384), BF),
            pltpu.VMEM((2, 2, 256, 384), BF),
            pltpu.VMEM((2, 16, 64, 384), BF),
            pltpu.VMEM((HPD, KD, 128), F32),
            pltpu.VMEM((HPD, 256, 128), F32),
            pltpu.VMEM((HPD, 64, 128), F32),
            pltpu.VMEM((3, SHARE, 256), BF),
            pltpu.VMEM((NH, SHARE, 256), BF),
            pltpu.VMEM((8, 128), jnp.int32),
            pltpu.VMEM((NS, 8, 128), jnp.int32),
            pltpu.VMEM((NH, D, D), BF),
            pltpu.VMEM((NH, D, D), BF),
            pltpu.VMEM((NH, 192, D), BF),
            dma, dma, dma, dma((4,)), dma((4, 4)), dma((4, 4)), dma((3, 7)), dma((3, 7)), dma((3,)),
            dma((2,)), dma((2,)), dma((2,)), dma((2,)), dma((3,)), dma((3,)),
        ],
        compiler_params=pltpu.CompilerParams(
            collective_id=0, has_side_effects=True, vmem_limit_bytes=56 * 1024 * 1024
        ),
        cost_estimate=pl.CostEstimate(flops=12_000_000_000, bytes_accessed=20_000_000, transcendentals=5_000_000),
    )(
        kept_tiles, middle_head_offset, far_head_offset, kept_tiles.reshape(KD, 1), tile_features,
        attn_gain.reshape(1, D), wqkv, mlp_gain.reshape(1, D), up_weight, down_weight, out_weight,
    )


def solution(mesh):
    in_specs = (
        P(("seq", "head"), None),
        P("seq"),
        P(),
        P(None, None, "head"),
        P("head", None),
        P("head"),
        P("head"),
        P(),
        P(None, "head"),
        P("head", None),
    )
    out_specs = P(("seq", "head"), None)
    return jax.shard_map(local, mesh=mesh, in_specs=in_specs, out_specs=out_specs, check_vma=False)
```

profile of v0, /device:TPU:0, one launch (start us, length us, event | category | flops | bytes accessed | tf_op | source)
XLA Modules:
  0.0 114.6 jit_solution(17030525379247244726)
XLA Ops:
  0.0 1.3 %fusion = (bf16[768,1,1,64]{0,3,2,1:T(8,128)(2,1)S(1)}, bf16[768,1,1,64]{0,3,2,1:T(8,128)(2,1)S(1)}, bf16[768,1,1,64]{0,3,2,1:T(8,128)(2,1)S(1)}, bf16[768,1,1,6...) fusion(bf16[768,3,3,64]{0,3,2,1:T(8,128)(2,1)} %bitcast.11), kind=kLoop, calls=%fused_computation | loop fusion | bytes 1769472 | tf_op jit(solution)/shard_map/slice | solution.py:386
  1.3 0.2 copy.29
  1.5 0.2 copy.21
  1.6 0.2 copy.22
  1.8 0.2 copy.23
  2.0 0.2 copy.24
  2.2 0.2 copy.25
  2.3 0.2 copy.26
  2.5 0.2 copy.27
  2.7 0.2 copy.28
  2.9 0.0 copy-start
  2.9 0.0 copy-start.1
  3.0 0.0 copy-start.2
  3.0 2.1 %concatenate.7.wqkv = bf16[768,768]{1,0:T(8,128)(2,1)} concatenate(bf16[768,64]{1,0:T(8,128)(2,1)S(1)} %broadcast_in_dim.3, bf16[768,64]{1,0:T(8,128)(2,1)S(1)} %bitcast.13, bf16[768,64]{1,0:T(8,128)(2,1)S(1)} %bitcast.14, bf16[768,128]{1,0:T(8,128)(2,1)S(1)} %concatenate.6, bf16[768,64]{1,0:T(8,128)(2,1)S(1)} %bitcast.15, bf16[768,64]{1,0:T(8,128)(2,1)S(1)} %bitcast.16, ...), dimensions={1} | concatenate | bytes 2359296 | tf_op jit(solution)/shard_map/concatenate | solution.py:387
  5.1 0.0 copy-done
  5.1 1.1 copy.20.kept_c
  6.1 0.0 copy-done.1
  6.1 0.6 reshape.13.again
  6.7 0.0 copy-done.2
  6.7 0.6 reshape.15.mgain
  7.3 105.5 %shard_map.100 = bf16[256,768]{1,0:T(8,128)(2,1)} custom-call(s32[1024]{0:T(1024)} %kept_s.1, s32[3]{0:T(128)} %moff.1, s32[3]{0:T(128)} %foff.1, s32[1024,1]{1,0:T(8,128)} %copy.20.kept_c, bf16[640,768]{1,0:T(8,128)(2,1)} %feat.1, f32[1,768]{1,0:T(1,128)} %reshape.13.again, bf16[768,768]{1,0:T(8,128)(2,1)} %concatenate.7.wqkv, f32[1,768]{1,0:T(1,128)} %reshape.15.mgain, ...), custom_call_target="tpu_custom_call" | custom-call | flops 12000000000 | bytes 20000000 | tf_op jit(solution)/shard_map/pallas_call | solution.py:392
  112.8 1.8 %copy.31 = bf16[256,768]{1,0:T(8,128)(2,1)} copy(bf16[256,768]{1,0:T(8,128)(2,1)} %shard_map.100) | data formatting | bytes 786432
  (2 shorter events, 0.1 us)
Async XLA Ops:
  2.9 2.1 %copy-start = (s32[1024]{0:T(1024)S(1)}, s32[1024]{0:T(1024)}, u32[]{:S(2)}) copy-start(s32[1024]{0:T(1024)} %kept_s.1) | copy-start | bytes 12292
  2.9 3.2 %copy-start.1 = (f32[768]{0:T(1024)S(1)}, f32[768]{0:T(1024)}, u32[]{:S(2)}) copy-start(f32[768]{0:T(1024)} %param.12) | copy-start | bytes 9220
  3.0 3.8 %copy-start.2 = (f32[768]{0:T(1024)S(1)}, f32[768]{0:T(1024)}, u32[]{:S(2)}) copy-start(f32[768]{0:T(1024)} %param.17) | copy-start | bytes 9220
where the time goes:
time: 116 us; the launch traced here: 115 us
  Pallas kernels  105 us (91%)
  local copies, waits for them, and re-layouts  9 us (8%)
    pallas_call x1, Pallas kernels, local(): pl.pallas_call(kernel, out_shape=jax.ShapeDtypeStruct((SHARE, D), BF), in...  105 us
    unnamed x16, local copies, waits for them, and re-layouts  3.3 us

commit v1 on v0

v1 whole, which is shorter than its diff:
```python
import functools

import jax
import jax.numpy as jnp
from jax import lax
from jax.experimental import pallas as pl
from jax.experimental.pallas import tpu as pltpu
from jax.sharding import PartitionSpec as P

NS = 32
NH = 4
ND = NS * NH
D = 768
KD = 1024
HD = 64
HPD = 3
WIN = 16
ROWS = 640
SHARE = KD // NH
EPS = 1e-05
NEG = -1e30
BF = jnp.bfloat16
F32 = jnp.float32


def dot(a, b):
    return lax.dot_general(a, b, (((1,), (0,)), ((), ())), preferred_element_type=F32)


def dot_nt(a, b):
    return lax.dot_general(a, b, (((1,), (1,)), ((), ())), preferred_element_type=F32)


def layer_norm(x, gain):
    centred = x - jnp.mean(x, axis=-1, keepdims=True)
    variance = jnp.mean(centred * centred, axis=-1, keepdims=True)
    return centred * lax.rsqrt(variance + EPS) * gain


def iota(shape, axis):
    return lax.broadcasted_iota(jnp.int32, shape, axis)


def v_first(head):
    return head != 1


def kernel(
    moff, foff, kept8, again6, mgain6, feat_in, qkv_in, up, down, outw,
    o_ref,
    feat, wraw, wqkv, send, recv, slot, dense, q, kv, qmid, qfar, normed, midkv, farkv, acc, accm, accf,
    ho_send, ho_recv, fk_send, fk_recv, upf, downf, outf,
    fk_ss, fk_rs, s1_ss, s1_rs, xs, xr, os, orr, bs, br, wl, ls, ms, mr, fs, fr, hs, hr,
):
    me = lax.axis_index("seq")
    h = lax.axis_index("head")
    right, left, opp = (h + 1) % NH, (h + 3) % NH, (h + 2) % NH
    core = me % 2
    chip = me // 2
    sib = me + 1 - 2 * core
    zbit = chip % 2
    zpart = me + 2 - 4 * zbit
    source = me * NH + h
    ypos, zpos = chip // 4, chip % 4
    a = ypos * (1 - core) + zpos * core
    b = zpos * (1 - core) + ypos * core
    a_next, a_prev, b_next, b_prev, b_opp = (a + 1) % 4, (a + 3) % 4, (b + 1) % 4, (b + 3) % 4, (b + 2) % 4

    def along(da, db):
        y = (ypos + (1 - core) * da + core * db) % 4
        z = (zpos + core * da + (1 - core) * db) % 4
        return (y * 4 + z) * 2 + core


    def rcopy(src, dst, ssem, rsem, seq, head):
        return pltpu.make_async_remote_copy(
            src_ref=src, dst_ref=dst, send_sem=ssem, recv_sem=rsem,
            device_id=(seq, head), device_id_type=pl.DeviceIdType.MESH,
        )

    feat_load = pltpu.make_async_copy(feat_in, feat, ls.at[0])
    feat_load.start()
    qkv_load = pltpu.make_async_copy(qkv_in, wraw, ls.at[1])
    qkv_load.start()
    again = jnp.concatenate([again6[k:k + 1] for k in range(6)], axis=1)
    mgain = jnp.concatenate([mgain6[k:k + 1] for k in range(6)], axis=1)

    barrier = pltpu.get_barrier_semaphore()

    def greet(i, c):
        pl.semaphore_signal(barrier, inc=1, device_id=((me + i) % NS, h), device_id_type=pl.DeviceIdType.MESH)
        return c

    lax.fori_loop(1, NS, greet, 0)
    for other in (right, left, opp):
        pl.semaphore_signal(barrier, inc=1, device_id=(me, other), device_id_type=pl.DeviceIdType.MESH)
    first = kept8[0:1, 0:1]
    fk_send[...] = jnp.broadcast_to(first, (8, 128))
    fk_recv[0] = fk_send[...]
    pl.semaphore_wait(barrier, NS - 1 + NH - 1)

    def send_first(i, c):
        rcopy(fk_send, fk_recv.at[(NS - i) % 4 * 8 + (NS - i) // 4], fk_ss, fk_rs, (me + i) % NS, h).start()
        return c

    lax.fori_loop(1, NS, send_first, 0)

    out_local = pltpu.make_async_copy(outw, outf.at[h], wl.at[2])
    lo = pl.multiple_of(core * 96, 16)
    own = pl.ds(lo, 96)
    out_mine = [
        rcopy(outw.at[own], outf.at[h, own], os.at[0], orr.at[0], me, right),
        rcopy(outw.at[own], outf.at[h, own], os.at[1], orr.at[1], me, left),
    ]
    at_l, at_r = pl.ds(lo, 48), pl.ds(pl.multiple_of(core * 96 + 48, 16), 48)
    out_ahead = [
        rcopy(outf.at[left, at_l], outf.at[left, at_l], os.at[2], orr.at[2], me, right),
        rcopy(outf.at[right, at_r], outf.at[right, at_r], os.at[3], orr.at[3], me, left),
    ]
    out_twin = [
        rcopy(outf.at[f, own], outf.at[f, own], os.at[4 + k], orr.at[4 + k], sib, h)
        for k, f in enumerate((left, right, opp))
    ]

    def eighth(at, skip, count):
        return pl.ds(pl.multiple_of(core * 384 + at * 96 + skip, 16), count)

    half = pl.ds(pl.multiple_of(core * 384, 16), 384)
    big_local, big_x1, big_x2, big_a1, big_a2, big_twin = [], [], [], [[], [], []], [[], [], []], [[], [], []]
    for w, (inp, full) in enumerate(((up, upf), (down, downf))):
        def same(f, rows, k, seq, head):
            return rcopy(full.at[f, rows], full.at[f, rows], bs.at[w, k], br.at[w, k], seq, head)

        big_local.append(pltpu.make_async_copy(inp, full.at[h], wl.at[w]))
        mine = eighth(a, 0, 96)
        for k, other in enumerate((right, left)):
            big_x1.append(rcopy(inp.at[mine], full.at[h, mine], bs.at[w, k], br.at[w, k], me, other))
        big_x2.append(same(left, eighth(a, 0, 48), 2, me, right))
        big_x2.append(same(right, eighth(a, 48, 48), 3, me, left))
        for k, f in enumerate((left, right, opp)):
            big_a1[k].append(same(f, mine, 4 + k, along(1, 0), h))
            big_a1[k].append(same(f, mine, 7 + k, along(3, 0), h))
            big_a2[k].append(same(f, eighth(a_prev, 0, 48), 10 + k, along(1, 0), h))
            big_a2[k].append(same(f, eighth(a_next, 48, 48), 13 + k, along(3, 0), h))
            big_twin[k].append(same(f, half, 16 + k, sib, h))

    def start(copies):
        for copy in copies:
            copy.start()
            drains.append(copy.wait_send)

    def arrived(copies):
        for copy in copies:
            copy.wait_recv()

    drains = [lambda: all_first.wait_send()]
    for copy in [out_local] + big_local:
        copy.start()
    start(out_mine)
    start(big_x1)

    for r in range(KD // 128):
        kc = jnp.broadcast_to(kept8[r:r + 1], (128, 128)).T
        sender = kc & (ND - 1)
        s_seq, s_head = lax.shift_right_arithmetic(sender, 2), sender & (NH - 1)
        within = lax.shift_right_arithmetic(kc, 7) - lax.shift_right_arithmetic(first - sender + (ND - 1), 7)
        rel = (me - s_seq + NS) & (NS - 1)
        slot[r * 128:(r + 1) * 128] = (
            (rel & 3) * 32 + s_head * 8 + lax.shift_right_arithmetic(rel, 2)
        ) * WIN + within

    all_first = rcopy(fk_recv.at[pl.ds(1, NS - 1)], fk_recv.at[pl.ds(1, NS - 1)], fk_ss, fk_rs, me, right)
    all_first.wait_recv()

    feat_load.wait()

    def send_windows(g):
        start = lax.shift_right_arithmetic(fk_recv[g * 8:g * 8 + 8] - source + (ND - 1), 7)
        start = jnp.concatenate([start, start], axis=1).reshape(128, 128)
        want = start + iota((128, 128), 0) % WIN - iota((128, 128), 1)
        pick = jnp.concatenate(
            [(want == t * 128).astype(F32).astype(BF) for t in range(ROWS // 128)], axis=1
        )
        send[g * 128:(g + 1) * 128] = dot(pick, feat[...]).astype(BF)

        def one(i, c):
            rcopy(
                send.at[pl.ds(pl.multiple_of(g * 128 + i * WIN, WIN), WIN)],
                recv.at[g, h, pl.ds(pl.multiple_of(i * WIN, WIN), WIN)],
                s1_ss, s1_rs.at[g], (me + 4 * i + g) % NS, h,
            ).start()
            return c

        lax.fori_loop(1 if g == 0 else 0, 8, one, 0)
        if g == 0:
            recv[0, h, 0:WIN] = send[0:WIN]

    sent = send.at[pl.ds(WIN, (NS - 1) * WIN)]
    drains.append(lambda: rcopy(sent, sent, s1_ss, s1_rs.at[0], me, right).wait_send())

    def arrive(g):
        lo = WIN if g == 0 else 0
        part = recv.at[g, h, pl.ds(lo, 128 - lo)]
        rcopy(part, part, s1_ss, s1_rs.at[g], me, right).wait_recv()

    rings = []
    for g in range(4):
        rings.append((
            rcopy(recv.at[g, h], recv.at[g, h], xs.at[g, 0], xr.at[g, 0], me, right),
            rcopy(recv.at[g, h], recv.at[g, h], xs.at[g, 1], xr.at[g, 1], me, left),
            rcopy(recv.at[g, left, pl.ds(0, 64)], recv.at[g, left, pl.ds(0, 64)], xs.at[g, 2], xr.at[g, 2], me, right),
            rcopy(recv.at[g, right, pl.ds(64, 64)], recv.at[g, right, pl.ds(64, 64)], xs.at[g, 3], xr.at[g, 3], me, left),
        ))

    def compact(g):
        rings[g][2].wait_recv()
        rings[g][3].wait_recv()

        def block(b, c):
            at = pl.ds(pl.multiple_of(b * 256, 256), 256)
            want = slot[at] - g * 512 - iota((256, 128), 1)
            pick = jnp.concatenate([(want == t * 128).astype(F32).astype(BF) for t in range(4)], axis=1)
            got = dot(pick, recv[g].reshape(512, D))
            if g == 0:
                dense[at] = got
            else:
                dense[at] = dense[at] + got
            return c

        lax.fori_loop(0, KD // 256, block, 0)

    def ring_pass(g):
        rings[g][0].wait_recv()
        rings[g][2].start()
        rings[g][1].wait_recv()
        rings[g][3].start()

    drains += [copy.wait_send for ring in rings for copy in ring]
    def ring_start(g):
        arrive(g)
        rings[g][0].start()
        rings[g][1].start()

    send_windows(0)
    send_windows(1)
    ring_start(0)
    send_windows(2)
    ring_start(1)
    send_windows(3)
    ring_pass(0)
    qkv_load.wait()
    for j in range(HPD):
        low, high = j * 128, j * 128 + 64
        rows = slice(j * 64, j * 64 + 64)
        at_q, at_0 = (high, low) if v_first(j) else (low, high)
        wqkv[at_0:at_0 + 64] = jnp.zeros((64, D), BF)
        wqkv[at_q:at_q + 64] = (wraw[0, rows].astype(F32) * 0.125).astype(BF)
        wqkv[384 + at_q:384 + at_q + 64] = wraw[1, rows]
        wqkv[384 + at_0:384 + at_0 + 64] = wraw[2, rows]
    ring_start(2)
    ring_pass(1)
    arrived(big_x1)
    start(big_a1[0] + big_a1[1])
    ring_start(3)
    ring_pass(2)
    compact(0)
    ring_pass(3)
    start(big_x2)
    arrived(out_mine)
    start(out_ahead + out_twin[:2])
    arrived(big_a1[0] + big_a1[1])
    start(big_a2[0] + big_a2[1])
    compact(1)
    compact(2)
    compact(3)

    def project_kv(blk, c):
        at = pl.ds(pl.multiple_of(blk * 256, 256), 256)
        block = layer_norm(dense[at], again).astype(BF)
        normed[at] = block
        kvb = dot_nt(block, wqkv[384:]).astype(BF)
        kv[at] = kvb
        at_m = pl.ds(pl.multiple_of(blk * 64, 64), 64)
        at_f = pl.ds(pl.multiple_of(blk * 16, 16), 16)
        for j in range(HPD):
            cols = slice(j * 128, (j + 1) * 128)
            sel = (iota((64, 256), 1) == iota((64, 256), 0) * 4 + moff[j]).astype(F32).astype(BF)
            midkv[core, zbit, at_m, cols] = dot(sel, kvb[:, cols]).astype(BF)
            sel = (iota((16, 256), 1) == iota((16, 256), 0) * 16 + foff[j]).astype(F32).astype(BF)
            farkv[core, b, a, at_f, cols] = dot(sel, kvb[:, cols]).astype(BF)
        return c

    lax.fori_loop(0, KD // 256, project_kv, 0)

    def far_copy(at, k, seq):
        return rcopy(farkv.at[at], farkv.at[at], fs.at[k], fr.at[k], seq, h)

    far_a1 = [far_copy((core, b, a), 0, along(1, 0)), far_copy((core, b, a), 1, along(3, 0))]
    far_a2 = [
        far_copy((core, b, a_prev, pl.ds(0, 32)), 2, along(1, 0)),
        far_copy((core, b, a_next, pl.ds(32, 32)), 3, along(3, 0)),
    ]
    far_b1 = [far_copy((core, b), 4, along(0, 1)), far_copy((core, b), 5, along(0, 3))]
    far_b2 = [
        far_copy((core, b_prev, pl.ds(0, 2)), 6, along(0, 1)),
        far_copy((core, b_next, pl.ds(2, 2)), 7, along(0, 3)),
    ]
    far_twin = [far_copy((core, at), 8 + k, sib) for k, at in enumerate((b, b_prev, b_next, b_opp))]
    mid_z = rcopy(midkv.at[core, zbit], midkv.at[core, zbit], ms.at[0], mr.at[0], zpart, h)
    mid_s = rcopy(midkv.at[core], midkv.at[core], ms.at[1], mr.at[1], sib, h)
    start(far_a1)
    start([mid_z])

    def project_q(blk, c):
        at = pl.ds(pl.multiple_of(blk * 256, 256), 256)
        qb = dot_nt(normed[at], wqkv[:384]).astype(BF)
        q[at] = qb
        at_m = pl.ds(pl.multiple_of(blk * 64, 64), 64)
        at_f = pl.ds(pl.multiple_of(blk * 16, 16), 16)
        for j in range(HPD):
            cols = slice(j * 128, (j + 1) * 128)
            sel = (iota((64, 256), 1) == iota((64, 256), 0) * 4 + moff[j]).astype(F32).astype(BF)
            qmid[at_m, cols] = dot(sel, qb[:, cols]).astype(BF)
            sel = (iota((16, 256), 1) == iota((16, 256), 0) * 16 + foff[j]).astype(F32).astype(BF)
            qfar[at_f, cols] = dot(sel, qb[:, cols]).astype(BF)
        return c

    lax.fori_loop(0, KD // 256, project_q, 0)
    arrived(far_a1)
    start(far_a2)

    def attend(qb, keys, j):
        scores = dot_nt(qb, keys)
        top = jnp.max(scores, axis=-1, keepdims=True)
        p = jnp.exp(scores - top)
        total = jnp.sum(p, axis=-1, keepdims=True)
        out = dot(p.astype(BF), keys)
        lane = iota(out.shape, 1)
        base = 64 if v_first(j) else 0
        out = jnp.where((lane >= base) & (lane < base + 32), top, out)
        return jnp.where((lane >= base + 32) & (lane < base + 64), total, out)

    def short(j, first_block):
        cols = slice(j * 128, (j + 1) * 128)

        def block(blk, c):
            at = pl.ds(pl.multiple_of(blk * 256, 256), 256)
            acc[j, at] = attend(q[at, cols], kv[:, cols], j)
            return c

        lax.fori_loop(first_block, first_block + 2, block, 0)

    short(0, 0)
    arrived(far_a2)
    start(far_b1 + far_twin[:1])
    arrived(big_x2)
    start(big_a1[2])
    arrived(big_a2[0] + big_a2[1])
    start(big_twin[0] + big_twin[1])
    short(0, 2)
    short(1, 0)
    arrived(far_b1)
    start(far_b2 + far_twin[1:3])
    short(1, 2)
    arrived([mid_z])
    start([mid_s])
    arrived(big_a1[2])
    start(big_a2[2])
    short(2, 0)
    arrived(far_b2)
    start(far_twin[3:])
    arrived(out_ahead)
    start(out_twin[2:])
    short(2, 2)
    arrived(big_a2[2])
    start(big_twin[2])
    arrived([mid_s])
    for j in range(HPD):
        cols = slice(j * 128, (j + 1) * 128)
        accm[j] = attend(qmid[:, cols], midkv[:, :, :, cols].reshape(KD, 128), j)
    arrived(far_twin)
    for j in range(HPD):
        cols = slice(j * 128, (j + 1) * 128)
        accf[j] = attend(qfar[:, cols], farkv[:, :, :, :, cols].reshape(2048, 128), j)

    def spread(one_hot, x):
        one = x.astype(BF)
        rest = x - one.astype(F32)
        two = rest.astype(BF)
        three = (rest - two.astype(F32)).astype(BF)
        return dot(one_hot, one) + dot(one_hot, two) + dot(one_hot, three)

    def merge(g):
        heads = []
        at = pl.ds(pl.multiple_of(g * 256, 256), 256)
        at_m = pl.ds(pl.multiple_of(g * 64, 64), 64)
        at_f = pl.ds(pl.multiple_of(g * 16, 16), 16)
        for j in range(HPD):
            base = 64 if v_first(j) else 0
            near = acc[j, at]
            hot_m = (iota((256, 64), 0) == iota((256, 64), 1) * 4 + moff[j]).astype(F32).astype(BF)
            hot_f = (iota((256, 16), 0) == iota((256, 16), 1) * 16 + foff[j]).astype(F32).astype(BF)
            middle = spread(hot_m, accm[j, at_m])
            far = spread(hot_f, accf[j, at_f])
            pos = iota((256, 1), 0)
            in_m = pos % 4 == moff[j]
            in_f = pos % 16 == foff[j]
            top_n = near[:, base:base + 1]
            top_m = jnp.where(in_m, middle[:, base:base + 1], NEG)
            top_f = jnp.where(in_f, far[:, base:base + 1], NEG)
            top = jnp.maximum(jnp.maximum(top_n, top_m), top_f)
            c_n = jnp.exp(top_n - top)
            c_m = jnp.exp(top_m - top)
            c_f = jnp.exp(top_f - top)
            under = (
                c_n * near[:, base + 32:base + 33]
                + c_m * middle[:, base + 32:base + 33]
                + c_f * far[:, base + 32:base + 33]
            )
            heads.append((c_n * near + c_m * middle + c_f * far) / under)
        lane = iota((256, 128), 1)
        lower = jnp.where(lane < 64, heads[0], heads[1])
        third = heads[2]
        upper = jnp.where(lane[:128] < 64, third[:128], pltpu.roll(third[128:], 64, 1))
        return lower.astype(BF), upper.astype(BF)

    swaps = []
    for r, g in enumerate((opp, right, left)):
        ho_send[r, :256], ho_send[r, 256:] = merge(g)
        swap = rcopy(ho_send.at[r], ho_recv.at[h], hs.at[r], hr.at[r], me, g)
        start([swap])
        swaps.append(swap)
    ho_recv[h, :256], ho_recv[h, 256:] = merge(h)
    out_local.wait()
    arrived(out_twin)
    arrived(swaps)
    attended = jnp.zeros((SHARE, D), F32)
    lane = iota((128, 128), 1)
    for g in range(NH):
        third = ho_recv[g, 256:]
        zero = jnp.zeros_like(third)
        third = jnp.concatenate([jnp.where(lane < 64, third, zero), jnp.where(lane < 64, zero, third)], axis=0)
        tail = outf[g, 128:]
        product = dot(ho_recv[g, :256], outf[g, :128]) + dot(third, jnp.concatenate([tail, tail], axis=0))
        attended = attended + product.astype(BF).astype(F32)
    residual = dense[pl.ds(pl.multiple_of(h * SHARE, SHARE), SHARE)] + attended
    normed_two = layer_norm(residual, mgain).astype(BF)
    for copy in big_local:
        copy.wait()
    arrived(big_twin[0] + big_twin[1] + big_twin[2])

    def feed(g, total):
        hidden = dot(normed_two, upf[g])
        hidden = (0.5 * hidden * (1.0 + lax.erf(hidden * 0.7071067811865476))).astype(BF)
        return total + dot(hidden, downf[g]).astype(BF).astype(F32)

    o_ref[...] = (residual + lax.fori_loop(0, NH, feed, jnp.zeros((SHARE, D), F32))).astype(BF)

    for drain in drains:
        drain()


def local(tile_features, kept_tiles, attn_gain, qkv_weight, out_weight, middle_head_offset,
          far_head_offset, mlp_gain, up_weight, down_weight):
    vmem = pl.BlockSpec(memory_space=pltpu.VMEM)
    smem = pl.BlockSpec(memory_space=pltpu.SMEM)
    hbm = pl.BlockSpec(memory_space=pl.ANY)
    dma = pltpu.SemaphoreType.DMA
    return pl.pallas_call(
        kernel,
        out_shape=jax.ShapeDtypeStruct((SHARE, D), BF),
        in_specs=[smem, smem, vmem, vmem, vmem, hbm, hbm, hbm, hbm, hbm],
        out_specs=vmem,
        scratch_shapes=[
            pltpu.VMEM((ROWS, D), BF),
            pltpu.VMEM((3, 192, D), BF),
            pltpu.VMEM((D, D), BF),
            pltpu.VMEM((NS * WIN, D), BF),
            pltpu.VMEM((4, NH, 128, D), BF),
            pltpu.VMEM((KD, 128), jnp.int32),
            pltpu.VMEM((KD, D), F32),
            pltpu.VMEM((KD, 384), BF),
            pltpu.VMEM((KD, 384), BF),
            pltpu.VMEM((256, 384), BF),
            pltpu.VMEM((64, 384), BF),
            pltpu.VMEM((KD, D), BF),
            pltpu.VMEM((2, 2, 256, 384), BF),
            pltpu.VMEM((2, 4, 4, 64, 384), BF),
            pltpu.VMEM((HPD, KD, 128), F32),
            pltpu.VMEM((HPD, 256, 128), F32),
            pltpu.VMEM((HPD, 64, 128), F32),
            pltpu.VMEM((3, 384, 128), BF),
            pltpu.VMEM((NH, 384, 128), BF),
            pltpu.VMEM((8, 128), jnp.int32),
            pltpu.VMEM((NS, 8, 128), jnp.int32),
            pltpu.VMEM((NH, D, D), BF),
            pltpu.VMEM((NH, D, D), BF),
            pltpu.VMEM((NH, 192, D), BF),
            dma, dma, dma, dma((4,)), dma((4, 4)), dma((4, 4)), dma((7,)), dma((7,)), dma((2, 19)), dma((2, 19)),
            dma((3,)), dma((2,)), dma((2,)), dma((2,)), dma((12,)), dma((12,)), dma((3,)), dma((3,)),
        ],
        compiler_params=pltpu.CompilerParams(
            collective_id=0, has_side_effects=True, vmem_limit_bytes=56 * 1024 * 1024
        ),
        cost_estimate=pl.CostEstimate(flops=12_000_000_000, bytes_accessed=20_000_000, transcendentals=5_000_000),
    )(
        middle_head_offset, far_head_offset, kept_tiles.reshape(8, 128), attn_gain.reshape(6, 128),
        mlp_gain.reshape(6, 128), tile_features, qkv_weight.transpose(1, 2, 0), up_weight, down_weight, out_weight,
    )


def solution(mesh):
    in_specs = (
        P(("seq", "head"), None),
        P("seq"),
        P(),
        P(None, None, "head"),
        P("head", None),
        P("head"),
        P("head"),
        P(),
        P(None, "head"),
        P("head", None),
    )
    out_specs = P(("seq", "head"), None)
    return jax.shard_map(local, mesh=mesh, in_specs=in_specs, out_specs=out_specs, check_vma=False)
```

time: 116 us -> 92.9 us (0.80); the launches traced: 115 us -> 92.7 us
  Pallas kernels: 105 us -> 90.9 us
  local copies, waits for them, and re-layouts: 9 us -> 1.77 us
    pallas_call x1, Pallas kernels: 105 us -> 90.9 us  [local(): pl.pallas_call(kernel, out_shape=jax.ShapeDtypeStruct((SHARE, D), BF), in...]
    reshape x3 -> x0, local copies, waits for them, and re-layouts: 2.23 us -> none  [the longest x1 1.05 us: local(): kept_tiles.reshape(KD, 1)]
    concatenate x2 -> x0, local copies, waits for them, and re-layouts: 2.14 us -> none  [local(): wqkv = jnp.concatenate(columns, axis=1)]
    unnamed x16 -> x1, local copies, waits for them, and re-layouts: 3.3 us -> 1.77 us
    slice x1 -> x0, local copies, waits for them, and re-layouts: 1.3 us -> none  [local(): parts[:, 1, j]]
where the time goes in v1:
time: 92.9 us; the launch traced here: 92.7 us
  Pallas kernels  90.9 us (98%)
  local copies, waits for them, and re-layouts  1.77 us (2%)
    pallas_call x1, Pallas kernels, local(): pl.pallas_call(kernel, out_shape=jax.ShapeDtypeStruct((SHARE, D), BF), in...  90.9 us

profile of v1, /device:TPU:0, one launch (start us, length us, event | category | flops | bytes accessed | tf_op | source)
XLA Modules:
  0.0 92.7 jit_solution(12937290176619970466)
XLA Ops:
  0.0 90.9 %shard_map.100 = bf16[256,768]{1,0:T(8,128)(2,1)} custom-call(s32[3]{0:T(128)} %moff.1, s32[3]{0:T(128)} %foff.1, s32[8,128]{1,0:T(8,128)} %bitcast.5, f32[6,128]{1,0:T(8,128)} %bitcast.6, f32[6,128]{1,0:T(8,128)} %bitcast.7, bf16[640,768]{1,0:T(8,128)(2,1)} %feat_in.1, bf16[3,192,768]{2,1,0:T(8,128)(2,1)} %bitcast.4, bf16[768,768]{1,0:T(8,128)(2,1)} %up.1, ...), custom_call_target="tpu_custom_call" | custom-call | flops 12000000000 | bytes 20000000 | tf_op jit(solution)/shard_map/pallas_call | solution.py:469
  91.0 1.8 %copy.12 = bf16[256,768]{1,0:T(8,128)(2,1)} copy(bf16[256,768]{1,0:T(8,128)(2,1)} %shard_map.100) | data formatting | bytes 786432

commit v2 on v1

--- a/solution.py
+++ b/solution.py
@@ -15,10 +15,18 @@
 HD = 64
 HPD = 3
 WIN = 16
+GROUPS = 8
+PER = NS // GROUPS
+GROWS = PER * WIN
 ROWS = 640
 SHARE = KD // NH
 EPS = 1e-05
 NEG = -1e30
+CHIPS = (
+    (0, 0), (0, 1), (0, 3), (1, 0), (3, 0), (1, 1), (1, 3), (3, 1),
+    (3, 3), (0, 2), (2, 0), (1, 2), (2, 1), (2, 3), (3, 2), (2, 2),
+)
+PLACES = tuple((dy, dz, dc) for dy, dz in CHIPS for dc in (0, 1))
 BF = jnp.bfloat16
 F32 = jnp.float32
 
@@ -48,7 +56,7 @@
 def kernel(
     moff, foff, kept8, again6, mgain6, feat_in, qkv_in, up, down, outw,
     o_ref,
-    feat, wraw, wqkv, send, recv, slot, dense, q, kv, qmid, qfar, normed, midkv, farkv, acc, accm, accf,
+    feat, wraw, wqkv, send, recv, slot, dense, q, kv, qmid, qfar, normed, nfar, midkv, farkv, acc, accm, accf,
     ho_send, ho_recv, fk_send, fk_recv, upf, downf, outf,
     fk_ss, fk_rs, s1_ss, s1_rs, xs, xr, os, orr, bs, br, wl, ls, ms, mr, fs, fr, hs, hr,
 ):
@@ -72,6 +80,10 @@
         return (y * 4 + z) * 2 + core
 
 
+    def offset(n, sign):
+        dy, dz, dc = PLACES[n]
+        return ((ypos + sign * dy) % 4 * 4 + (zpos + sign * dz) % 4) * 2 + (core + dc) % 2
+
     def rcopy(src, dst, ssem, rsem, seq, head):
         return pltpu.make_async_remote_copy(
             src_ref=src, dst_ref=dst, send_sem=ssem, recv_sem=rsem,
@@ -87,11 +99,8 @@
 
     barrier = pltpu.get_barrier_semaphore()
 
-    def greet(i, c):
-        pl.semaphore_signal(barrier, inc=1, device_id=((me + i) % NS, h), device_id_type=pl.DeviceIdType.MESH)
-        return c
-
-    lax.fori_loop(1, NS, greet, 0)
+    for n in range(1, NS):
+        pl.semaphore_signal(barrier, inc=1, device_id=(offset(n, 1), h), device_id_type=pl.DeviceIdType.MESH)
     for other in (right, left, opp):
         pl.semaphore_signal(barrier, inc=1, device_id=(me, other), device_id_type=pl.DeviceIdType.MESH)
     first = kept8[0:1, 0:1]
@@ -99,11 +108,8 @@
     fk_recv[0] = fk_send[...]
     pl.semaphore_wait(barrier, NS - 1 + NH - 1)
 
-    def send_first(i, c):
-        rcopy(fk_send, fk_recv.at[(NS - i) % 4 * 8 + (NS - i) // 4], fk_ss, fk_rs, (me + i) % NS, h).start()
-        return c
-
-    lax.fori_loop(1, NS, send_first, 0)
+    for n in range(1, NS):
+        rcopy(fk_send, fk_recv.at[n], fk_ss, fk_rs.at[n // PER], offset(n, 1), h).start()
 
     out_local = pltpu.make_async_copy(outw, outf.at[h], wl.at[2])
     lo = pl.multiple_of(core * 96, 16)
@@ -153,10 +159,10 @@
         for copy in copies:
             copy.wait_recv()
 
-    drains = [lambda: all_first.wait_send()]
+    all_first = fk_recv.at[pl.ds(1, NS - 1)]
+    drains = [lambda: rcopy(all_first, all_first, fk_ss, fk_rs.at[0], me, right).wait_send()]
     for copy in [out_local] + big_local:
         copy.start()
-    start(out_mine)
     start(big_x1)
 
     for r in range(KD // 128):
@@ -164,34 +170,35 @@
         sender = kc & (ND - 1)
         s_seq, s_head = lax.shift_right_arithmetic(sender, 2), sender & (NH - 1)
         within = lax.shift_right_arithmetic(kc, 7) - lax.shift_right_arithmetic(first - sender + (ND - 1), 7)
-        rel = (me - s_seq + NS) & (NS - 1)
+        way = (lax.shift_right_arithmetic(s_seq, 3) - ypos) & 3
+        way = way * 4 + ((lax.shift_right_arithmetic(s_seq, 1) - zpos) & 3)
+        words = [sum(CHIPS.index(divmod(8 * half + k, 4)) << (4 * k) for k in range(7)) for half in (0, 1)]
+        last = [CHIPS.index(divmod(8 * half + 7, 4)) for half in (0, 1)]
+        place = lax.shift_right_arithmetic(jnp.where(way < 8, words[0], words[1]), (way & 7) * 4) & 15
+        place = jnp.where((way & 7) == 7, jnp.where(way < 8, last[0], last[1]), place)
+        rel = place * 2 + ((s_seq + core) & 1)
         slot[r * 128:(r + 1) * 128] = (
-            (rel & 3) * 32 + s_head * 8 + lax.shift_right_arithmetic(rel, 2)
+            lax.shift_right_arithmetic(rel, 2) * (PER * NH) + s_head * PER + (rel & (PER - 1))
         ) * WIN + within
 
-    all_first = rcopy(fk_recv.at[pl.ds(1, NS - 1)], fk_recv.at[pl.ds(1, NS - 1)], fk_ss, fk_rs, me, right)
-    all_first.wait_recv()
-
     feat_load.wait()
 
     def send_windows(g):
-        start = lax.shift_right_arithmetic(fk_recv[g * 8:g * 8 + 8] - source + (ND - 1), 7)
-        start = jnp.concatenate([start, start], axis=1).reshape(128, 128)
-        want = start + iota((128, 128), 0) % WIN - iota((128, 128), 1)
+        lo = 1 if g == 0 else 0
+        firsts = fk_recv.at[pl.ds(g * PER + lo, PER - lo)]
+        rcopy(firsts, firsts, fk_ss, fk_rs.at[g], me, right).wait_recv()
+        start = lax.shift_right_arithmetic(fk_recv[g * PER:(g + 1) * PER] - source + (ND - 1), 7)
+        start = jnp.concatenate([start, start], axis=1).reshape(GROWS, 128)
+        want = start + iota((GROWS, 128), 0) % WIN - iota((GROWS, 128), 1)
         pick = jnp.concatenate(
             [(want == t * 128).astype(F32).astype(BF) for t in range(ROWS // 128)], axis=1
         )
-        send[g * 128:(g + 1) * 128] = dot(pick, feat[...]).astype(BF)
-
-        def one(i, c):
+        send[g * GROWS:(g + 1) * GROWS] = dot(pick, feat[...]).astype(BF)
+        for i in range(lo, PER):
             rcopy(
-                send.at[pl.ds(pl.multiple_of(g * 128 + i * WIN, WIN), WIN)],
-                recv.at[g, h, pl.ds(pl.multiple_of(i * WIN, WIN), WIN)],
-                s1_ss, s1_rs.at[g], (me + 4 * i + g) % NS, h,
+                send.at[pl.ds(g * GROWS + i * WIN, WIN)], recv.at[g, h, pl.ds(i * WIN, WIN)],
+                s1_ss, s1_rs.at[g], offset(g * PER + i, -1), h,
             ).start()
-            return c
-
-        lax.fori_loop(1 if g == 0 else 0, 8, one, 0)
         if g == 0:
             recv[0, h, 0:WIN] = send[0:WIN]
 
@@ -200,27 +207,28 @@
 
     def arrive(g):
         lo = WIN if g == 0 else 0
-        part = recv.at[g, h, pl.ds(lo, 128 - lo)]
+        part = recv.at[g, h, pl.ds(lo, GROWS - lo)]
         rcopy(part, part, s1_ss, s1_rs.at[g], me, right).wait_recv()
 
     rings = []
-    for g in range(4):
+    for g in range(GROUPS):
         rings.append((
             rcopy(recv.at[g, h], recv.at[g, h], xs.at[g, 0], xr.at[g, 0], me, right),
             rcopy(recv.at[g, h], recv.at[g, h], xs.at[g, 1], xr.at[g, 1], me, left),
-            rcopy(recv.at[g, left, pl.ds(0, 64)], recv.at[g, left, pl.ds(0, 64)], xs.at[g, 2], xr.at[g, 2], me, right),
-            rcopy(recv.at[g, right, pl.ds(64, 64)], recv.at[g, right, pl.ds(64, 64)], xs.at[g, 3], xr.at[g, 3], me, left),
+            rcopy(recv.at[g, left, pl.ds(0, GROWS // 2)], recv.at[g, left, pl.ds(0, GROWS // 2)], xs.at[g, 2], xr.at[g, 2], me, right),
+            rcopy(recv.at[g, right, pl.ds(GROWS // 2, GROWS // 2)], recv.at[g, right, pl.ds(GROWS // 2, GROWS // 2)], xs.at[g, 3], xr.at[g, 3], me, left),
         ))
 
     def compact(g):
-        rings[g][2].wait_recv()
-        rings[g][3].wait_recv()
+        for k in (2 * g, 2 * g + 1):
+            rings[k][2].wait_recv()
+            rings[k][3].wait_recv()
 
         def block(b, c):
             at = pl.ds(pl.multiple_of(b * 256, 256), 256)
             want = slot[at] - g * 512 - iota((256, 128), 1)
             pick = jnp.concatenate([(want == t * 128).astype(F32).astype(BF) for t in range(4)], axis=1)
-            got = dot(pick, recv[g].reshape(512, D))
+            got = dot(pick, recv[2 * g:2 * g + 2].reshape(512, D))
             if g == 0:
                 dense[at] = got
             else:
@@ -247,7 +255,18 @@
     send_windows(2)
     ring_start(1)
     send_windows(3)
+    send_windows(4)
     ring_pass(0)
+    ring_start(2)
+    send_windows(5)
+    send_windows(6)
+    ring_pass(1)
+    ring_start(3)
+    send_windows(7)
+    ring_pass(2)
+    ring_start(4)
+    arrived(big_x1)
+    start(big_a1[0] + big_a1[1])
     qkv_load.wait()
     for j in range(HPD):
         low, high = j * 128, j * 128 + 64
@@ -257,77 +276,100 @@
         wqkv[at_q:at_q + 64] = (wraw[0, rows].astype(F32) * 0.125).astype(BF)
         wqkv[384 + at_q:384 + at_q + 64] = wraw[1, rows]
         wqkv[384 + at_0:384 + at_0 + 64] = wraw[2, rows]
-    ring_start(2)
-    ring_pass(1)
-    arrived(big_x1)
-    start(big_a1[0] + big_a1[1])
-    ring_start(3)
-    ring_pass(2)
+    ring_pass(3)
+    ring_start(5)
+    ring_pass(4)
+    ring_start(6)
+    ring_pass(5)
+    ring_start(7)
     compact(0)
-    ring_pass(3)
-    start(big_x2)
-    arrived(out_mine)
-    start(out_ahead + out_twin[:2])
     arrived(big_a1[0] + big_a1[1])
     start(big_a2[0] + big_a2[1])
+    ring_pass(6)
     compact(1)
+    ring_pass(7)
+    start(big_x2)
+    start(out_mine)
+    arrived(big_a2[0] + big_a2[1])
+    start(big_twin[0] + big_twin[1])
     compact(2)
     compact(3)
 
-    def project_kv(blk, c):
-        at = pl.ds(pl.multiple_of(blk * 256, 256), 256)
-        block = layer_norm(dense[at], again).astype(BF)
-        normed[at] = block
-        kvb = dot_nt(block, wqkv[384:]).astype(BF)
-        kv[at] = kvb
-        at_m = pl.ds(pl.multiple_of(blk * 64, 64), 64)
-        at_f = pl.ds(pl.multiple_of(blk * 16, 16), 16)
+    def norm(blk, c):
+        block = layer_norm(dense[pl.ds(pl.multiple_of(blk * 256, 256), 256)], again).astype(BF)
+        normed[pl.ds(pl.multiple_of(blk * 256, 256), 256)] = block
+        row = iota((48, 256), 0)
+        which = jnp.where(row < 16, foff[0], jnp.where(row < 32, foff[1], foff[2]))
+        sel = (iota((48, 256), 1) == (row & 15) * 16 + which).astype(F32).astype(BF)
+        rows = dot(sel, block).astype(BF)
         for j in range(HPD):
-            cols = slice(j * 128, (j + 1) * 128)
-            sel = (iota((64, 256), 1) == iota((64, 256), 0) * 4 + moff[j]).astype(F32).astype(BF)
-            midkv[core, zbit, at_m, cols] = dot(sel, kvb[:, cols]).astype(BF)
-            sel = (iota((16, 256), 1) == iota((16, 256), 0) * 16 + foff[j]).astype(F32).astype(BF)
-            farkv[core, b, a, at_f, cols] = dot(sel, kvb[:, cols]).astype(BF)
+            nfar[j, pl.ds(pl.multiple_of(blk * 16, 16), 16)] = rows[j * 16:(j + 1) * 16]
         return c
 
-    lax.fori_loop(0, KD // 256, project_kv, 0)
+    lax.fori_loop(0, KD // 256, norm, 0)
+    for j in range(HPD):
+        cols = slice(j * 128, (j + 1) * 128)
+        farkv[core, b, a, :, cols] = dot_nt(nfar[j], wqkv[384 + j * 128:512 + j * 128]).astype(BF)
 
     def far_copy(at, k, seq):
         return rcopy(farkv.at[at], farkv.at[at], fs.at[k], fr.at[k], seq, h)
 
+    a_opp = (a + 2) % 4
+    spots = (a, a_prev, a_next, a_opp)
     far_a1 = [far_copy((core, b, a), 0, along(1, 0)), far_copy((core, b, a), 1, along(3, 0))]
     far_a2 = [
         far_copy((core, b, a_prev, pl.ds(0, 32)), 2, along(1, 0)),
         far_copy((core, b, a_next, pl.ds(32, 32)), 3, along(3, 0)),
     ]
-    far_b1 = [far_copy((core, b), 4, along(0, 1)), far_copy((core, b), 5, along(0, 3))]
+    far_b1 = [
+        [far_copy((core, b, x), 4 + 2 * k, along(0, 1)), far_copy((core, b, x), 5 + 2 * k, along(0, 3))]
+        for k, x in enumerate(spots)
+    ]
     far_b2 = [
-        far_copy((core, b_prev, pl.ds(0, 2)), 6, along(0, 1)),
-        far_copy((core, b_next, pl.ds(2, 2)), 7, along(0, 3)),
+        [
+            far_copy((core, b_prev, x, pl.ds(0, 32)), 12 + 2 * k, along(0, 1)),
+            far_copy((core, b_next, x, pl.ds(32, 32)), 13 + 2 * k, along(0, 3)),
+        ]
+        for k, x in enumerate(spots)
     ]
-    far_twin = [far_copy((core, at), 8 + k, sib) for k, at in enumerate((b, b_prev, b_next, b_opp))]
+    far_twin = [far_copy((core, at), 20 + k, sib) for k, at in enumerate((b, b_prev, b_next, b_opp))]
     mid_z = rcopy(midkv.at[core, zbit], midkv.at[core, zbit], ms.at[0], mr.at[0], zpart, h)
     mid_s = rcopy(midkv.at[core], midkv.at[core], ms.at[1], mr.at[1], sib, h)
-    start(far_a1)
+    start(far_a1 + far_b1[0])
+
+    def project_kv(blk, c):
+        at = pl.ds(pl.multiple_of(blk * 256, 256), 256)
+        kvb = dot_nt(normed[at], wqkv[384:]).astype(BF)
+        kv[at] = kvb
+        at_m = pl.ds(pl.multiple_of(blk * 64, 64), 64)
+        for j in range(HPD):
+            cols = slice(j * 128, (j + 1) * 128)
+            sel = (iota((64, 256), 1) == iota((64, 256), 0) * 4 + moff[j]).astype(F32).astype(BF)
+            midkv[core, zbit, at_m, cols] = dot(sel, kvb[:, cols]).astype(BF)
+        return c
+
+    lax.fori_loop(0, KD // 256, project_kv, 0)
     start([mid_z])
+    arrived(far_a1)
+    start(far_a2 + far_b1[1] + far_b1[2])
 
     def project_q(blk, c):
         at = pl.ds(pl.multiple_of(blk * 256, 256), 256)
         qb = dot_nt(normed[at], wqkv[:384]).astype(BF)
         q[at] = qb
         at_m = pl.ds(pl.multiple_of(blk * 64, 64), 64)
-        at_f = pl.ds(pl.multiple_of(blk * 16, 16), 16)
         for j in range(HPD):
             cols = slice(j * 128, (j + 1) * 128)
             sel = (iota((64, 256), 1) == iota((64, 256), 0) * 4 + moff[j]).astype(F32).astype(BF)
             qmid[at_m, cols] = dot(sel, qb[:, cols]).astype(BF)
-            sel = (iota((16, 256), 1) == iota((16, 256), 0) * 16 + foff[j]).astype(F32).astype(BF)
-            qfar[at_f, cols] = dot(sel, qb[:, cols]).astype(BF)
         return c
 
     lax.fori_loop(0, KD // 256, project_q, 0)
-    arrived(far_a1)
-    start(far_a2)
+    for j in range(HPD):
+        cols = slice(j * 128, (j + 1) * 128)
+        qfar[:, cols] = dot_nt(nfar[j], wqkv[j * 128:(j + 1) * 128]).astype(BF)
+    arrived(far_a2 + far_b1[0])
+    start(far_b1[3] + far_b2[0] + far_twin[:1])
 
     def attend(qb, keys, j):
         scores = dot_nt(qb, keys)
@@ -350,30 +392,27 @@
 
         lax.fori_loop(first_block, first_block + 2, block, 0)
 
+    arrived(out_mine)
+    start(out_ahead + out_twin[:2])
     short(0, 0)
-    arrived(far_a2)
-    start(far_b1 + far_twin[:1])
-    arrived(big_x2)
-    start(big_a1[2])
-    arrived(big_a2[0] + big_a2[1])
-    start(big_twin[0] + big_twin[1])
     short(0, 2)
+    arrived(far_b1[1] + far_b1[2])
+    start(far_b2[1] + far_b2[2])
     short(1, 0)
-    arrived(far_b1)
-    start(far_b2 + far_twin[1:3])
+    arrived(far_b1[3])
+    start(far_b2[3] + far_twin[1:3])
     short(1, 2)
     arrived([mid_z])
     start([mid_s])
-    arrived(big_a1[2])
-    start(big_a2[2])
-    short(2, 0)
-    arrived(far_b2)
-    start(far_twin[3:])
     arrived(out_ahead)
     start(out_twin[2:])
+    short(2, 0)
+    for k in range(4):
+        arrived(far_b2[k])
+    start(far_twin[3:])
+    arrived(big_x2)
+    start(big_a1[2])
     short(2, 2)
-    arrived(big_a2[2])
-    start(big_twin[2])
     arrived([mid_s])
     for j in range(HPD):
         cols = slice(j * 128, (j + 1) * 128)
@@ -383,6 +422,8 @@
         cols = slice(j * 128, (j + 1) * 128)
         accf[j] = attend(qfar[:, cols], farkv[:, :, :, :, cols].reshape(2048, 128), j)
 
+    arrived(big_a1[2])
+    start(big_a2[2])
     def spread(one_hot, x):
         one = x.astype(BF)
         rest = x - one.astype(F32)
@@ -431,6 +472,8 @@
         start([swap])
         swaps.append(swap)
     ho_recv[h, :256], ho_recv[h, 256:] = merge(h)
+    arrived(big_a2[2])
+    start(big_twin[2])
     out_local.wait()
     arrived(out_twin)
     arrived(swaps)
@@ -449,12 +492,12 @@
         copy.wait()
     arrived(big_twin[0] + big_twin[1] + big_twin[2])
 
-    def feed(g, total):
+    total = residual
+    for g in range(NH):
         hidden = dot(normed_two, upf[g])
         hidden = (0.5 * hidden * (1.0 + lax.erf(hidden * 0.7071067811865476))).astype(BF)
-        return total + dot(hidden, downf[g]).astype(BF).astype(F32)
-
-    o_ref[...] = (residual + lax.fori_loop(0, NH, feed, jnp.zeros((SHARE, D), F32))).astype(BF)
+        total = total + dot(hidden, downf[g]).astype(BF).astype(F32)
+    o_ref[...] = total.astype(BF)
 
     for drain in drains:
         drain()
@@ -476,7 +519,7 @@
             pltpu.VMEM((3, 192, D), BF),
             pltpu.VMEM((D, D), BF),
             pltpu.VMEM((NS * WIN, D), BF),
-            pltpu.VMEM((4, NH, 128, D), BF),
+            pltpu.VMEM((GROUPS, NH, GROWS, D), BF),
             pltpu.VMEM((KD, 128), jnp.int32),
             pltpu.VMEM((KD, D), F32),
             pltpu.VMEM((KD, 384), BF),
@@ -484,6 +527,7 @@
             pltpu.VMEM((256, 384), BF),
             pltpu.VMEM((64, 384), BF),
             pltpu.VMEM((KD, D), BF),
+            pltpu.VMEM((HPD, 64, D), BF),
             pltpu.VMEM((2, 2, 256, 384), BF),
             pltpu.VMEM((2, 4, 4, 64, 384), BF),
             pltpu.VMEM((HPD, KD, 128), F32),
@@ -496,8 +540,8 @@
             pltpu.VMEM((NH, D, D), BF),
             pltpu.VMEM((NH, D, D), BF),
             pltpu.VMEM((NH, 192, D), BF),
-            dma, dma, dma, dma((4,)), dma((4, 4)), dma((4, 4)), dma((7,)), dma((7,)), dma((2, 19)), dma((2, 19)),
-            dma((3,)), dma((2,)), dma((2,)), dma((2,)), dma((12,)), dma((12,)), dma((3,)), dma((3,)),
+            dma, dma((GROUPS,)), dma, dma((GROUPS,)), dma((GROUPS, 4)), dma((GROUPS, 4)), dma((7,)), dma((7,)), dma((2, 19)), dma((2, 19)),
+            dma((3,)), dma((2,)), dma((2,)), dma((2,)), dma((24,)), dma((24,)), dma((3,)), dma((3,)),
         ],
         compiler_params=pltpu.CompilerParams(
             collective_id=0, has_side_effects=True, vmem_limit_bytes=56 * 1024 * 1024

time: 92.9 us -> 86.4 us (0.930)
  Pallas kernels: 90.9 us -> 84.3 us
    pallas_call x1, Pallas kernels: 90.9 us -> 84.3 us  [local(): pl.pallas_call(kernel, out_shape=jax.ShapeDtypeStruct((SHARE, D), BF), in...]
where the time goes in v2:
time: 86.4 us; the launch traced here: 86.1 us
  Pallas kernels  84.3 us (98%)
  local copies, waits for them, and re-layouts  1.77 us (2%)
    pallas_call x1, Pallas kernels, local(): pl.pallas_call(kernel, out_shape=jax.ShapeDtypeStruct((SHARE, D), BF), in...  84.3 us
    unnamed x1, local copies, waits for them, and re-layouts  1.77 us

profile of v2, /device:TPU:0, one launch (start us, length us, event | category | flops | bytes accessed | tf_op | source)
XLA Modules:
  0.0 86.1 jit_solution(1568093432234377079)
XLA Ops:
  0.0 84.3 %shard_map.100 = bf16[256,768]{1,0:T(8,128)(2,1)} custom-call(s32[3]{0:T(128)} %moff.1, s32[3]{0:T(128)} %foff.1, s32[8,128]{1,0:T(8,128)} %bitcast.5, f32[6,128]{1,0:T(8,128)} %bitcast.6, f32[6,128]{1,0:T(8,128)} %bitcast.7, bf16[640,768]{1,0:T(8,128)(2,1)} %feat_in.1, bf16[3,192,768]{2,1,0:T(8,128)(2,1)} %bitcast.4, bf16[768,768]{1,0:T(8,128)(2,1)} %up.1, ...), custom_call_target="tpu_custom_call" | custom-call | flops 12000000000 | bytes 20000000 | tf_op jit(solution)/shard_map/pallas_call | solution.py:512
  84.3 1.8 %copy.12 = bf16[256,768]{1,0:T(8,128)(2,1)} copy(bf16[256,768]{1,0:T(8,128)(2,1)} %shard_map.100) | data formatting | bytes 786432

commit v3 on v2

--- a/solution.py
+++ b/solution.py
@@ -56,7 +56,7 @@
 def kernel(
     moff, foff, kept8, again6, mgain6, feat_in, qkv_in, up, down, outw,
     o_ref,
-    feat, wraw, wqkv, send, recv, slot, dense, q, kv, qmid, qfar, normed, nfar, midkv, farkv, acc, accm, accf,
+    feat, wraw, wqkv, wturn, send, recv, slot, dense, q, kv, qmid, qfar, normed, nfar, midkv, farkv, acc, accm, accf,
     ho_send, ho_recv, fk_send, fk_recv, upf, downf, outf,
     fk_ss, fk_rs, s1_ss, s1_rs, xs, xr, os, orr, bs, br, wl, ls, ms, mr, fs, fr, hs, hr,
 ):
@@ -79,6 +79,11 @@
         z = (zpos + core * da + (1 - core) * db) % 4
         return (y * 4 + z) * 2 + core
 
+
+    y_next, y_prev, z_next, z_prev = (ypos + 1) % 4, (ypos + 3) % 4, (zpos + 1) % 4, (zpos + 3) % 4
+
+    def across(dy, dz):
+        return ((ypos + dy) % 4 * 4 + (zpos + dz) % 4) * 2 + core
 
     def offset(n, sign):
         dy, dz, dc = PLACES[n]
@@ -225,8 +230,8 @@
             rings[k][3].wait_recv()
 
         def block(b, c):
-            at = pl.ds(pl.multiple_of(b * 256, 256), 256)
-            want = slot[at] - g * 512 - iota((256, 128), 1)
+            at = pl.ds(pl.multiple_of(b * 512, 512), 512)
+            want = slot[at] - g * 512 - iota((512, 128), 1)
             pick = jnp.concatenate([(want == t * 128).astype(F32).astype(BF) for t in range(4)], axis=1)
             got = dot(pick, recv[2 * g:2 * g + 2].reshape(512, D))
             if g == 0:
@@ -235,7 +240,7 @@
                 dense[at] = dense[at] + got
             return c
 
-        lax.fori_loop(0, KD // 256, block, 0)
+        lax.fori_loop(0, KD // 512, block, 0)
 
     def ring_pass(g):
         rings[g][0].wait_recv()
@@ -276,8 +281,16 @@
         wqkv[at_q:at_q + 64] = (wraw[0, rows].astype(F32) * 0.125).astype(BF)
         wqkv[384 + at_q:384 + at_q + 64] = wraw[1, rows]
         wqkv[384 + at_0:384 + at_0 + 64] = wraw[2, rows]
+
+    def turn(parts):
+        for k in parts:
+            at = slice(k * 128, (k + 1) * 128)
+            wturn[:, at] = wqkv[at].astype(F32).T.astype(BF)
+
+    turn((0, 1, 2))
     ring_pass(3)
     ring_start(5)
+    turn((3, 4, 5))
     ring_pass(4)
     ring_start(6)
     ring_pass(5)
@@ -309,65 +322,64 @@
     lax.fori_loop(0, KD // 256, norm, 0)
     for j in range(HPD):
         cols = slice(j * 128, (j + 1) * 128)
-        farkv[core, b, a, :, cols] = dot_nt(nfar[j], wqkv[384 + j * 128:512 + j * 128]).astype(BF)
+        farkv[core, ypos, zpos, :, cols] = dot(nfar[j], wturn[:, 384 + j * 128:512 + j * 128]).astype(BF)
 
     def far_copy(at, k, seq):
         return rcopy(farkv.at[at], farkv.at[at], fs.at[k], fr.at[k], seq, h)
 
-    a_opp = (a + 2) % 4
-    spots = (a, a_prev, a_next, a_opp)
-    far_a1 = [far_copy((core, b, a), 0, along(1, 0)), far_copy((core, b, a), 1, along(3, 0))]
+    spots = (zpos, z_prev, z_next, (zpos + 2) % 4)
+    far_a1 = [far_copy((core, ypos, zpos), 0, across(0, 1)), far_copy((core, ypos, zpos), 1, across(0, 3))]
     far_a2 = [
-        far_copy((core, b, a_prev, pl.ds(0, 32)), 2, along(1, 0)),
-        far_copy((core, b, a_next, pl.ds(32, 32)), 3, along(3, 0)),
+        far_copy((core, ypos, z_prev, pl.ds(0, 32)), 2, across(0, 1)),
+        far_copy((core, ypos, z_next, pl.ds(32, 32)), 3, across(0, 3)),
     ]
     far_b1 = [
-        [far_copy((core, b, x), 4 + 2 * k, along(0, 1)), far_copy((core, b, x), 5 + 2 * k, along(0, 3))]
+        [far_copy((core, ypos, x), 4 + 2 * k, across(1, 0)), far_copy((core, ypos, x), 5 + 2 * k, across(3, 0))]
         for k, x in enumerate(spots)
     ]
     far_b2 = [
         [
-            far_copy((core, b_prev, x, pl.ds(0, 32)), 12 + 2 * k, along(0, 1)),
-            far_copy((core, b_next, x, pl.ds(32, 32)), 13 + 2 * k, along(0, 3)),
+            far_copy((core, y_prev, x, pl.ds(0, 32)), 12 + 2 * k, across(1, 0)),
+            far_copy((core, y_next, x, pl.ds(32, 32)), 13 + 2 * k, across(3, 0)),
         ]
         for k, x in enumerate(spots)
     ]
-    far_twin = [far_copy((core, at), 20 + k, sib) for k, at in enumerate((b, b_prev, b_next, b_opp))]
+    far_twin = [far_copy((core, at), 20 + k, sib) for k, at in enumerate((ypos, y_prev, y_next, (ypos + 2) % 4))]
     mid_z = rcopy(midkv.at[core, zbit], midkv.at[core, zbit], ms.at[0], mr.at[0], zpart, h)
     mid_s = rcopy(midkv.at[core], midkv.at[core], ms.at[1], mr.at[1], sib, h)
     start(far_a1 + far_b1[0])
 
     def project_kv(blk, c):
-        at = pl.ds(pl.multiple_of(blk * 256, 256), 256)
-        kvb = dot_nt(normed[at], wqkv[384:]).astype(BF)
+        at = pl.ds(pl.multiple_of(blk * 512, 512), 512)
+        kvb = dot(normed[at], wturn[:, 384:]).astype(BF)
         kv[at] = kvb
-        at_m = pl.ds(pl.multiple_of(blk * 64, 64), 64)
+        at_m = pl.ds(pl.multiple_of(blk * 128, 128), 128)
         for j in range(HPD):
             cols = slice(j * 128, (j + 1) * 128)
-            sel = (iota((64, 256), 1) == iota((64, 256), 0) * 4 + moff[j]).astype(F32).astype(BF)
+            sel = (iota((128, 512), 1) == iota((128, 512), 0) * 4 + moff[j]).astype(F32).astype(BF)
             midkv[core, zbit, at_m, cols] = dot(sel, kvb[:, cols]).astype(BF)
         return c
 
-    lax.fori_loop(0, KD // 256, project_kv, 0)
+    lax.fori_loop(0, KD // 512, project_kv, 0)
     start([mid_z])
     arrived(far_a1)
     start(far_a2 + far_b1[1] + far_b1[2])
 
     def project_q(blk, c):
-        at = pl.ds(pl.multiple_of(blk * 256, 256), 256)
-        qb = dot_nt(normed[at], wqkv[:384]).astype(BF)
+        at = pl.ds(pl.multiple_of(blk * 512, 512), 512)
+        qb = dot(normed[at], wturn[:, :384]).astype(BF)
         q[at] = qb
-        at_m = pl.ds(pl.multiple_of(blk * 64, 64), 64)
+        at_m = pl.ds(pl.multiple_of(blk * 128, 128), 128)
         for j in range(HPD):
             cols = slice(j * 128, (j + 1) * 128)
-            sel = (iota((64, 256), 1) == iota((64, 256), 0) * 4 + moff[j]).astype(F32).astype(BF)
+            sel = (iota((128, 512), 1) == iota((128, 512), 0) * 4 + moff[j]).astype(F32).astype(BF)
             qmid[at_m, cols] = dot(sel, qb[:, cols]).astype(BF)
         return c
 
-    lax.fori_loop(0, KD // 256, project_q, 0)
+    lax.fori_loop(0, KD // 512, project_q, 0)
     for j in range(HPD):
         cols = slice(j * 128, (j + 1) * 128)
-        qfar[:, cols] = dot_nt(nfar[j], wqkv[j * 128:(j + 1) * 128]).astype(BF)
+        qfar[:, cols] = dot(nfar[j], wturn[:, j * 128:(j + 1) * 128]).astype(BF)
     arrived(far_a2 + far_b1[0])
     start(far_b1[3] + far_b2[0] + far_twin[:1])
 
@@ -385,12 +397,8 @@
     def short(j, first_block):
         cols = slice(j * 128, (j + 1) * 128)
 
-        def block(blk, c):
-            at = pl.ds(pl.multiple_of(blk * 256, 256), 256)
-            acc[j, at] = attend(q[at, cols], kv[:, cols], j)
-            return c
-
-        lax.fori_loop(first_block, first_block + 2, block, 0)
+        at = slice(first_block * 256, first_block * 256 + 512)
+        acc[j, at] = attend(q[at, cols], kv[:, cols], j)
 
     arrived(out_mine)
     start(out_ahead + out_twin[:2])
@@ -517,6 +525,7 @@
         scratch_shapes=[
             pltpu.VMEM((ROWS, D), BF),
             pltpu.VMEM((3, 192, D), BF),
+            pltpu.VMEM((D, D), BF),
             pltpu.VMEM((D, D), BF),
             pltpu.VMEM((NS * WIN, D), BF),
             pltpu.VMEM((GROUPS, NH, GROWS, D), BF),

time: 86.4 us -> 85.4 us (0.988)
  Pallas kernels: 84.3 us -> 82.8 us
    pallas_call x1, Pallas kernels: 84.3 us -> 82.8 us  [local(): pl.pallas_call(kernel, out_shape=jax.ShapeDtypeStruct((SHARE, D), BF), in...]
where the time goes in v3:
time: 85.4 us; the launch traced here: 84.6 us
  Pallas kernels  82.8 us (97%)
  local copies, waits for them, and re-layouts  1.77 us (2%)
    pallas_call x1, Pallas kernels, local(): pl.pallas_call(kernel, out_shape=jax.ShapeDtypeStruct((SHARE, D), BF), in...  82.8 us
    unnamed x1, local copies, waits for them, and re-layouts  1.77 us

profile of v3, /device:TPU:0, one launch (start us, length us, event | category | flops | bytes accessed | tf_op | source)
XLA Modules:
  0.0 84.6 jit_solution(16553941203058373724)
XLA Ops:
  0.0 82.8 %shard_map.100 = bf16[256,768]{1,0:T(8,128)(2,1)} custom-call(s32[3]{0:T(128)} %moff.1, s32[3]{0:T(128)} %foff.1, s32[8,128]{1,0:T(8,128)} %bitcast.5, f32[6,128]{1,0:T(8,128)} %bitcast.6, f32[6,128]{1,0:T(8,128)} %bitcast.7, bf16[640,768]{1,0:T(8,128)(2,1)} %feat_in.1, bf16[3,192,768]{2,1,0:T(8,128)(2,1)} %bitcast.4, bf16[768,768]{1,0:T(8,128)(2,1)} %up.1, ...), custom_call_target="tpu_custom_call" | custom-call | flops 12000000000 | bytes 20000000 | tf_op jit(solution)/shard_map/pallas_call | solution.py:520
  82.8 1.8 %copy.12 = bf16[256,768]{1,0:T(8,128)(2,1)} copy(bf16[256,768]{1,0:T(8,128)(2,1)} %shard_map.100) | data formatting | bytes 786432

commit v4 on v3

--- a/solution.py
+++ b/solution.py
@@ -430,8 +430,6 @@
         cols = slice(j * 128, (j + 1) * 128)
         accf[j] = attend(qfar[:, cols], farkv[:, :, :, :, cols].reshape(2048, 128), j)
 
-    arrived(big_a1[2])
-    start(big_a2[2])
     def spread(one_hot, x):
         one = x.astype(BF)
         rest = x - one.astype(F32)
@@ -479,15 +477,18 @@
         swap = rcopy(ho_send.at[r], ho_recv.at[h], hs.at[r], hr.at[r], me, g)
         start([swap])
         swaps.append(swap)
+        if r == 1:
+            arrived(big_a1[2])
+            start(big_a2[2])
     ho_recv[h, :256], ho_recv[h, 256:] = merge(h)
     arrived(big_a2[2])
     start(big_twin[2])
     out_local.wait()
     arrived(out_twin)
-    arrived(swaps)
     attended = jnp.zeros((SHARE, D), F32)
     lane = iota((128, 128), 1)
-    for g in range(NH):
+    for g, swap in ((h, []), (left, swaps[1:2]), (right, swaps[2:]), (opp, swaps[:1])):
+        arrived(swap)
         third = ho_recv[g, 256:]
         zero = jnp.zeros_like(third)
         third = jnp.concatenate([jnp.where(lane < 64, third, zero), jnp.where(lane < 64, zero, third)], axis=0)
@@ -498,10 +499,10 @@
     normed_two = layer_norm(residual, mgain).astype(BF)
     for copy in big_local:
         copy.wait()
-    arrived(big_twin[0] + big_twin[1] + big_twin[2])
 
     total = residual
-    for g in range(NH):
+    for g, twin in ((h, []), (left, big_twin[0]), (right, big_twin[1]), (opp, big_twin[2])):
+        arrived(twin)
         hidden = dot(normed_two, upf[g])
         hidden = (0.5 * hidden * (1.0 + lax.erf(hidden * 0.7071067811865476))).astype(BF)
         total = total + dot(hidden, downf[g]).astype(BF).astype(F32)

time: 85.4 us -> 84.7 us (level)
  no operation moved by 1% of the time
where the time goes in v4:
time: 84.7 us; the launch traced here: 84.6 us
  Pallas kernels  82.8 us (98%)
  local copies, waits for them, and re-layouts  1.77 us (2%)
    pallas_call x1, Pallas kernels, local(): pl.pallas_call(kernel, out_shape=jax.ShapeDtypeStruct((SHARE, D), BF), in...  82.8 us
    unnamed x1, local copies, waits for them, and re-layouts  1.77 us

profile of v4, /device:TPU:0, one launch (start us, length us, event | category | flops | bytes accessed | tf_op | source)
XLA Modules:
  0.0 84.6 jit_solution(6492222124432628648)
XLA Ops:
  0.0 82.8 %shard_map.100 = bf16[256,768]{1,0:T(8,128)(2,1)} custom-call(s32[3]{0:T(128)} %moff.1, s32[3]{0:T(128)} %foff.1, s32[8,128]{1,0:T(8,128)} %bitcast.5, f32[6,128]{1,0:T(8,128)} %bitcast.6, f32[6,128]{1,0:T(8,128)} %bitcast.7, bf16[640,768]{1,0:T(8,128)(2,1)} %feat_in.1, bf16[3,192,768]{2,1,0:T(8,128)(2,1)} %bitcast.4, bf16[768,768]{1,0:T(8,128)(2,1)} %up.1, ...), custom_call_target="tpu_custom_call" | custom-call | flops 12000000000 | bytes 20000000 | tf_op jit(solution)/shard_map/pallas_call | solution.py:521
  82.8 1.8 %copy.12 = bf16[256,768]{1,0:T(8,128)(2,1)} copy(bf16[256,768]{1,0:T(8,128)(2,1)} %shard_map.100) | data formatting | bytes 786432

commit v5 on v4

--- a/solution.py
+++ b/solution.py
@@ -481,8 +481,6 @@
             arrived(big_a1[2])
             start(big_a2[2])
     ho_recv[h, :256], ho_recv[h, 256:] = merge(h)
-    arrived(big_a2[2])
-    start(big_twin[2])
     out_local.wait()
     arrived(out_twin)
     attended = jnp.zeros((SHARE, D), F32)
@@ -495,6 +493,9 @@
         tail = outf[g, 128:]
         product = dot(ho_recv[g, :256], outf[g, :128]) + dot(third, jnp.concatenate([tail, tail], axis=0))
         attended = attended + product.astype(BF).astype(F32)
+        if not swap:
+            arrived(big_a2[2])
+            start(big_twin[2])
     residual = dense[pl.ds(pl.multiple_of(h * SHARE, SHARE), SHARE)] + attended
     normed_two = layer_norm(residual, mgain).astype(BF)
     for copy in big_local:

time: 84.7 us -> 84.7 us (level)
  no operation moved by 1% of the time
where the time goes in v5:
time: 84.7 us; the launch traced here: 84.6 us
  Pallas kernels  82.8 us (98%)
  local copies, waits for them, and re-layouts  1.77 us (2%)
    pallas_call x1, Pallas kernels, local(): pl.pallas_call(kernel, out_shape=jax.ShapeDtypeStruct((SHARE, D), BF), in...  82.8 us
    unnamed x1, local copies, waits for them, and re-layouts  1.77 us

profile of v5, /device:TPU:0, one launch (start us, length us, event | category | flops | bytes accessed | tf_op | source)
XLA Modules:
  0.0 84.6 jit_solution(12917877678543731217)
XLA Ops:
  0.0 82.8 %shard_map.100 = bf16[256,768]{1,0:T(8,128)(2,1)} custom-call(s32[3]{0:T(128)} %moff.1, s32[3]{0:T(128)} %foff.1, s32[8,128]{1,0:T(8,128)} %bitcast.5, f32[6,128]{1,0:T(8,128)} %bitcast.6, f32[6,128]{1,0:T(8,128)} %bitcast.7, bf16[640,768]{1,0:T(8,128)(2,1)} %feat_in.1, bf16[3,192,768]{2,1,0:T(8,128)(2,1)} %bitcast.4, bf16[768,768]{1,0:T(8,128)(2,1)} %up.1, ...), custom_call_target="tpu_custom_call" | custom-call | flops 12000000000 | bytes 20000000 | tf_op jit(solution)/shard_map/pallas_call | solution.py:522
  82.8 1.8 %copy.12 = bf16[256,768]{1,0:T(8,128)(2,1)} copy(bf16[256,768]{1,0:T(8,128)(2,1)} %shard_map.100) | data formatting | bytes 786432
